TPU v7x, 32 devices: a whole 2x2x4 slice. The times are simulated.
32 devices in a mesh: slab: 4 (over z), sub: 8 (over y, x, core).
Axes of the slice: x: 2, y: 2, z: 4, core: 2. Of those that a mesh axis runs over, the one named last changes fastest.
Arguments:
- velocity_field: float32 [3, 64, 256, 512], P(None, 'slab', 'sub'), may hold values from -6 to 6
- particle_state: float32 [1024, 6, 256], P(('slab', 'sub')), as said below
- stokes_time: float32 [1024, 256], P(('slab', 'sub')), may hold values from 0.2 to 2
- box_base: int32 [1024, 3], P(('slab', 'sub')), may hold values from -2 to 511, as said below
- live_bins: int32 [32], P(('slab', 'sub')), may hold values from 1 to 32, as said below
Outputs:
- state_out: float32 [1024, 6, 256], P(('slab', 'sub'))
Inputs may be any that keep to these rules, and one draw needn't show every extreme that they name: `box_base`: columns 0 and 1 lie from -2 to 14 and from -2 to 30, column 2 from 0 to 511; bin 0 has column 0 at -2 and column 2 at 511. `live_bins`: some device has all 32 slots occupied. `particle_state`: positions lie in the box's central cell, 0 to 1 in each coordinate.
All inputs are finite; a program needn't handle non-finite values.
Results may differ from a plain program's by a relative error of at most 0.0003.
Values sent between devices are 32-bit elements; how exact they have to be, the bound alone decides.
No kernel may reach another device: no remote copies, remote signals or barrier semaphores. Data moves between devices by JAX's collectives and lax.ppermute only.
A program may use at most 64 MiB of HBM per device.

v0:
```python
import jax
import jax.numpy as jnp
from jax import lax
from jax.sharding import PartitionSpec as P

SUBSTEPS = 4
GROUP = 8


STEP_SIZE = 0.2


def padded_2(shard, sides, width):
    for axis, dim in sides:
        devices, length = (lax.axis_size(axis), shard.shape[dim])
        up = [(i, (i + 1) % devices) for i in range(devices)]
        down = [(j, i) for i, j in up]
        last = lax.slice_in_dim(shard, length - width, length, axis=dim)
        first = lax.slice_in_dim(shard, 0, width, axis=dim)
        before = lax.ppermute(last, axis, up)
        after = lax.ppermute(first, axis, down)
        shard = jnp.concatenate([before, shard, after], axis=dim)
    return shard


def cubic_weights(offset):
    plus = offset + 1.0
    minus = offset - 1.0
    minus_two = offset - 2.0
    return jnp.stack(
        [
            -offset * minus * minus_two / 6.0,
            plus * minus * minus_two / 2.0,
            -plus * offset * minus_two / 2.0,
            plus * offset * minus / 6.0,
        ],
        axis=1,
    )


def sample(boxes, position):
    along_x = cubic_weights(position[:, 0])
    along_y = cubic_weights(position[:, 1])
    along_z = cubic_weights(position[:, 2])
    weights = (
        along_x[:, :, None, None, :] * along_y[:, None, :, None, :] * along_z[:, None, None, :, :]
    )
    return jnp.sum(boxes[:, :, :, :, :, None] * weights[:, None], axis=(2, 3, 4))


def advance(boxes, states, stokes):
    position = states[:, :3]
    velocity = states[:, 3:]
    rate = (1.0 / stokes)[:, None, :]
    for substep in range(SUBSTEPS):
        slope = (sample(boxes, position) - velocity) * rate
        middle_pos = position + 0.5 * STEP_SIZE * velocity
        middle_vel = velocity + 0.5 * STEP_SIZE * slope
        position = position + STEP_SIZE * middle_vel
        velocity = velocity + STEP_SIZE * (sample(boxes, middle_pos) - middle_vel) * rate
    return jnp.concatenate([position, velocity], axis=1)


def pick_boxes(grid, first_x, first_y, first_z):
    depth = grid.shape[3]
    offsets = jnp.arange(4, dtype=jnp.int32)
    cells_x = jnp.clip(first_x[:, None] + offsets[None, :], 0, grid.shape[1] - 1)
    cells_y = jnp.clip(first_y[:, None] + offsets[None, :], 0, grid.shape[2] - 1)
    cells_z = (first_z[:, None] + offsets[None, :]) % depth
    picked = grid[
        :, cells_x[:, :, None, None], cells_y[:, None, :, None], cells_z[:, None, None, :]
    ]
    return jnp.moveaxis(picked, 0, 1)


def body(velocity_field, particle_state, stokes_time, box_base, live_bins):
    live_count = live_bins[0]
    padded = padded_2(velocity_field, (("slab", 1), ("sub", 2)), 2)
    all_boxes = pick_boxes(padded, box_base[:, 0] + 2, box_base[:, 1] + 2, box_base[:, 2])

    def home_turn(index_turn, current):
        start = index_turn * GROUP
        states = lax.dynamic_slice_in_dim(particle_state, start, GROUP, 0)
        stokes = lax.dynamic_slice_in_dim(stokes_time, start, GROUP, 0)
        group_boxes = lax.dynamic_slice_in_dim(all_boxes, start, GROUP, 0)
        moved = advance(group_boxes, states, stokes)
        keep = start + jnp.arange(GROUP, dtype=jnp.int32) < live_count
        moved = jnp.where(keep[:, None, None], moved, states)
        return lax.dynamic_update_slice_in_dim(current, moved, start, 0)

    turn_count = (live_count + GROUP - 1) // GROUP
    return lax.fori_loop(jnp.int32(0), turn_count, home_turn, particle_state)


def solution(mesh):
    placed = (
        P(None, "slab", "sub", None),
        P(("slab", "sub"), None, None),
        P(("slab", "sub"), None),
        P(("slab", "sub"), None),
        P(("slab", "sub")),
    )
    return jax.shard_map(
        body, mesh=mesh, in_specs=placed, out_specs=P(("slab", "sub"), None, None), check_vma=False
    )
```

profile of v0, /device:TPU:21, one launch (start us, length us, event | category | flops | bytes accessed | tf_op | source)
XLA Modules:
  0.0 97.0 jit_solution(18160534063210117797)
XLA Ops:
  0.0 1.4 %fusion.180 = (f32[3,2,32,512]{3,2,1,0:T(8,128)S(1)}, f32[3,2,32,512]{3,2,1,0:T(8,128)S(1)}) fusion(f32[3,16,32,512]{3,2,1,0:T(8,128)} %param.7), kind=kLoop, calls=%fused_computation.360 | loop fusion | bytes 1572864 | tf_op jit(solution)/shard_map/slice | solution.py:19
  1.6 1.3 %collective-permute-start = (f32[3,2,32,512]{3,0,2,1:T(4,128)S(1)}, f32[3,2,32,512]{3,0,2,1:T(4,128)S(1)}, u32[]{:S(2)}, u32[]{:S(2)}) collective-permute-start(f32[3,2,32,512]{3,0,2,1:T(4,128)S(1)} %copy.69), channel_id=1, source_target_pairs={{0,8},{8,16},{16,24},{24,0},{1,9},{9,17},{17,25},{25,1},{2,10},{10... | collective-permute-start | bytes 1179656 | tf_op jit(solution)/shard_map/ppermute | solution.py:20
  3.6 11.0 %collective-permute-done = f32[3,2,32,512]{3,0,2,1:T(4,128)S(1)} collective-permute-done((f32[3,2,32,512]{3,0,2,1:T(4,128)S(1)}, f32[3,2,32,512]{3,0,2,1:T(4,128)S(1)}, u32[]{:S(2)}, u32[]{:S(2)}) %collective-permute-start) | collective-permute-done | bytes 393248 | tf_op jit(solution)/shard_map/ppermute | solution.py:20
  14.7 2.5 %copy_dynamic-update-slice_fusion = f32[3,20,32,512]{3,0,2,1:T(4,128)S(1)} fusion(f32[3,20,32,512]{3,0,2,1:T(4,128)S(1)} %constant_dynamic-update-slice_fusion.1, f32[3,16,32,512]{3,2,1,0:T(8,128)S(1)} %copy-done.1), kind=kLoop, calls=%fused_computation.340 | loop fusion | bytes 7340032
  17.2 8.5 %collective-permute-done.1 = f32[3,2,32,512]{3,0,2,1:T(4,128)S(1)} collective-permute-done((f32[3,2,32,512]{3,0,2,1:T(4,128)S(1)}, f32[3,2,32,512]{3,0,2,1:T(4,128)S(1)}, u32[]{:S(2)}, u32[]{:S(2)}) %collective-permute-start.1) | collective-permute-done | bytes 393248 | tf_op jit(solution)/shard_map/ppermute | solution.py:21
  25.8 2.4 %copy-done = f32[3,20,32,512]{3,0,2,1:T(4,128)} copy-done((f32[3,20,32,512]{3,0,2,1:T(4,128)}, f32[3,20,32,512]{3,0,2,1:T(4,128)S(1)}, u32[]{:S(2)}) %copy-start) | copy-done | bytes 3932184
  28.3 5.3 %collective-permute-start.2 = (f32[3,20,2,512]{3,0,2,1:T(4,128)S(1)}, f32[3,20,2,512]{3,0,2,1:T(4,128)S(1)}, u32[]{:S(2)}, u32[]{:S(2)}) collective-permute-start(f32[3,20,2,512]{3,0,2,1:T(4,128)S(1)} %get-tuple-element.311), channel_id=1, source_target_pairs={{0,1},{1,2},{2,3},{3,4},{4,5},{5,6},{6,7},{7,0},{8,9},{9,10},{10,1... | collective-permute-start | bytes 737288 | tf_op jit(solution)/shard_map/ppermute | solution.py:20
  34.9 4.4 %collective-permute-done.2 = f32[3,20,2,512]{3,0,2,1:T(4,128)S(1)} collective-permute-done((f32[3,20,2,512]{3,0,2,1:T(4,128)S(1)}, f32[3,20,2,512]{3,0,2,1:T(4,128)S(1)}, u32[]{:S(2)}, u32[]{:S(2)}) %collective-permute-start.2) | collective-permute-done | bytes 245792 | tf_op jit(solution)/shard_map/ppermute | solution.py:20
  39.4 2.7 %collective-permute-done.3 = f32[3,20,2,512]{3,0,2,1:T(4,128)S(1)} collective-permute-done((f32[3,20,2,512]{3,0,2,1:T(4,128)S(1)}, f32[3,20,2,512]{3,0,2,1:T(4,128)S(1)}, u32[]{:S(2)}, u32[]{:S(2)}) %collective-permute-start.3) | collective-permute-done | bytes 245792 | tf_op jit(solution)/shard_map/ppermute | solution.py:21
  42.1 7.1 %pad_maximum_fusion.24 = f32[3,20,36,512]{3,0,2,1:T(4,128)} fusion(f32[3,20,2,512]{3,0,2,1:T(4,128)S(1)} %collective-permute-done.3, f32[3,20,32,512]{3,0,2,1:T(4,128)} %copy-done, f32[3,20,2,512]{3,0,2,1:T(4,128)S(1)} %collective-permute-done.2), kind=kLoop, calls=%fused_computation.335 | loop fusion | flops 2211840 | bytes 8847360 | tf_op jit(solution)/shard_map/concatenate | solution.py:22
  49.2 28.2 %gather_fusion = f32[2048,3]{0,1:T(4,128)S(1)} fusion(f32[3,20,36,512]{3,0,2,1:T(4,128)} %pad_maximum_fusion.24, s32[2048]{0:T(1024)S(1)} %reshape.142), kind=kCustom, calls=%fused_computation | custom fusion | bytes 73728 | tf_op jit(solution)/shard_map/gather | solution.py:70
  77.4 1.0 %reshape.145 = f32[32,4,4,4,3]{3,2,1,0,4:T(4,128)S(1)} reshape(f32[2048,3]{0,1:T(4,128)S(1)} %gather_fusion) | data formatting | bytes 49152 | tf_op jit(solution)/shard_map/gather | solution.py:70
  78.4 0.5 copy.67
  78.9 17.4 %while.13 = (s32[]{:T(128)}, f32[32,6,256]{2,0,1:T(8,128)S(1)}, s32[]{:T(128)}, s32[]{:T(128)}, f32[32,6,256]{2,0,1:T(8,128)S(1)}, /*index=5*/f32[32,3,4,4,4]{0,...) while((s32[]{:T(128)}, f32[32,6,256]{2,0,1:T(8,128)S(1)}, ...), condition=%wide.region_9.10_spmd, body=%wide.region_0.9_spmd.sunk | while | flops 9375769 | bytes 15289103 | solution.py:92
  79.4 0.7 broadcast_multiply_fusion.34
  81.1 0.3 multiply_reduce_fusion.15
  82.5 0.7 add_compare_fusion.2
  83.8 0.7 broadcast_multiply_fusion.34
  86.9 0.7 add_compare_fusion.2
  88.1 0.7 broadcast_multiply_fusion.34
  91.2 0.7 add_compare_fusion.2
  92.5 0.7 broadcast_multiply_fusion.34
  95.6 0.7 add_compare_fusion.2
  96.3 0.7 copy-done.3
  (268 shorter events, 11.6 us)
Async XLA Ops:
  0.0 14.7 %copy-start.1 = (f32[3,16,32,512]{3,2,1,0:T(8,128)S(1)}, f32[3,16,32,512]{3,2,1,0:T(8,128)}, u32[]{:S(2)}) copy-start(f32[3,16,32,512]{3,2,1,0:T(8,128)} %param.7) | copy-start | bytes 9437188
  0.0 3.5 %copy-start.4 = (s32[32,3]{0,1:T(4,128)S(1)}, s32[32,3]{0,1:T(4,128)}, u32[]{:S(2)}) copy-start(s32[32,3]{0,1:T(4,128)} %param.10) | copy-start | bytes 1156
  1.6 12.9 %collective-permute-start = (f32[3,2,32,512]{3,0,2,1:T(4,128)S(1)}, f32[3,2,32,512]{3,0,2,1:T(4,128)S(1)}, u32[]{:S(2)}, u32[]{:S(2)}) collective-permute-start(f32[3,2,32,512]{3,0,2,1:T(4,128)S(1)} %copy.69), channel_id=1, source_target_pairs={{0,8},{8,16},{16,24},{24,0},{1,9},{9,17},{17,25},{25,1},{2,10},{10... | collective-permute-start | bytes 1179656 | tf_op jit(solution)/shard_map/ppermute | solution.py:20
  3.3 22.4 %collective-permute-start.1 = (f32[3,2,32,512]{3,0,2,1:T(4,128)S(1)}, f32[3,2,32,512]{3,0,2,1:T(4,128)S(1)}, u32[]{:S(2)}, u32[]{:S(2)}) collective-permute-start(f32[3,2,32,512]{3,0,2,1:T(4,128)S(1)} %copy.70), channel_id=1, source_target_pairs={{8,0},{16,8},{24,16},{0,24},{9,1},{17,9},{25,17},{1,25},{10,2},{18... | collective-permute-start | bytes 1179656 | tf_op jit(solution)/shard_map/ppermute | solution.py:21
  14.7 20.2 %copy-start.2 = (f32[32,6,256]{2,0,1:T(8,128)S(1)}, f32[32,6,256]{2,0,1:T(8,128)}, u32[]{:S(2)}) copy-start(f32[32,6,256]{2,0,1:T(8,128)} %param.8) | copy-start | bytes 589828
  25.8 2.4 %copy-start = (f32[3,20,32,512]{3,0,2,1:T(4,128)}, f32[3,20,32,512]{3,0,2,1:T(4,128)S(1)}, u32[]{:S(2)}) copy-start(f32[3,20,32,512]{3,0,2,1:T(4,128)S(1)} %constant_dynamic-update-slice_fusion) | copy-start | bytes 11796484
  28.3 11.1 %collective-permute-start.2 = (f32[3,20,2,512]{3,0,2,1:T(4,128)S(1)}, f32[3,20,2,512]{3,0,2,1:T(4,128)S(1)}, u32[]{:S(2)}, u32[]{:S(2)}) collective-permute-start(f32[3,20,2,512]{3,0,2,1:T(4,128)S(1)} %get-tuple-element.311), channel_id=1, source_target_pairs={{0,1},{1,2},{2,3},{3,4},{4,5},{5,6},{6,7},{7,0},{8,9},{9,10},{10,1... | collective-permute-start | bytes 737288 | tf_op jit(solution)/shard_map/ppermute | solution.py:20
  33.6 8.5 %collective-permute-start.3 = (f32[3,20,2,512]{3,0,2,1:T(4,128)S(1)}, f32[3,20,2,512]{3,0,2,1:T(4,128)S(1)}, u32[]{:S(2)}, u32[]{:S(2)}) collective-permute-start(f32[3,20,2,512]{3,0,2,1:T(4,128)S(1)} %get-tuple-element.312), channel_id=1, source_target_pairs={{1,0},{2,1},{3,2},{4,3},{5,4},{6,5},{7,6},{0,7},{9,8},{10,9},{11,1... | collective-permute-start | bytes 737288 | tf_op jit(solution)/shard_map/ppermute | solution.py:21
  96.3 0.7 copy-start.3
where the time goes:
time: 98 us; the launch traced here: 97 us
  local copies, waits for them, and re-layouts  38.2 us (39%)
  waiting for transfers between devices  26.7 us (27%)
  other arithmetic  22.5 us (23%)
  starting transfers between devices  6.92 us (7%)
  loops' own time  1.93 us (2%)
    gather x2, local copies, waits for them, and re-layouts, pick_boxes(): grid[:, cells_x[:, :, None, None], cells_y[:, None, :, None], cells_z[:,...  29.2 us
    ppermute x2, waiting for transfers between devices, padded_2(): before = lax.ppermute(last, axis, up)  15.4 us
    ppermute x2, waiting for transfers between devices, padded_2(): after = lax.ppermute(first, axis, down)  11.2 us
    concatenate x1, other arithmetic, padded_2(): shard = jnp.concatenate([before, shard, after], axis=dim)  7.05 us
    ppermute x2, starting transfers between devices, padded_2(): before = lax.ppermute(last, axis, up)  6.69 us
    unnamed x15, local copies, waits for them, and re-layouts  6.16 us
    reduce_sum x20, other arithmetic, sample(): jnp.sum(boxes[:, :, :, :, :, None] * weights[:, None], axis=(2, 3, 4))  5.63 us
    mul x4, other arithmetic, advance(): STEP_SIZE * (sample(boxes, middle_pos) - middle_vel) * rate  2.83 us
  transfers between devices with their start and end apart: 4, of which 4 were waited for; matrix products, arithmetic and copies ran while one was open for 4% of the time, Pallas kernels for 0%

commit v1 on v0

v1 whole, which is shorter than its diff:
```python
import functools

import jax
import jax.numpy as jnp
import numpy as np
from jax import lax
from jax.experimental import pallas as pl
from jax.experimental.pallas import tpu as pltpu
from jax.sharding import PartitionSpec as P

SUBSTEPS = 4
STEP_SIZE = 0.2
LANES = 128
NODES = 16
BLOCK = 8
TOP = 8
VMEM_LIMIT = 48 * 1024 * 1024


def lane_nodes():
    row = lax.broadcasted_iota(jnp.int32, (8, LANES), 0)
    lane = lax.broadcasted_iota(jnp.int32, (8, LANES), 1)
    return jnp.where(row < 4, lane // 4, -1000)


def flatten_rows(rows):
    return jnp.sum(pltpu.roll(rows, 0, 1, stride=4, stride_axis=0), axis=0, keepdims=True)


def gather_rows(padded, index, first_y, first_z, slot, nodes, lane, valid):
    tile = first_z // LANES
    offset = first_z % LANES
    tiles = padded.shape[-3]
    here = padded[(*index, tile, pl.ds(TOP + first_y, 8), slice(None))]
    there = padded[(*index, (tile + 1) % tiles, pl.ds(TOP + first_y, 8), slice(None))]
    rows = jnp.where(lane >= offset, here, there)
    rows = pltpu.roll(rows, (NODES * slot - first_z) & (LANES - 1), 1)
    wanted = jnp.where(valid, 4 * slot, -5000)
    return jnp.where(nodes == wanted, rows, 0.0)


def fill_halo(padded, before, after, plane_pairs, length):
    tiles = padded.shape[-3]
    for into, source in plane_pairs:
        for tile in range(tiles):
            lanes = slice(tile * LANES, (tile + 1) * LANES)
            padded[(*into, tile, slice(TOP - 2, TOP), slice(None))] = before[(*source, slice(None), lanes)]
            padded[(*into, tile, slice(TOP + length, TOP + length + 2), slice(None))] = after[
                (*source, slice(None), lanes)
            ]


def answer_kernel(upper_table, lower_table, field, before, after, upper_out, lower_out, edge, acc, hits, sems):
    comps, depth, length, cells = field.shape
    tiles = cells // LANES
    bins = upper_table.shape[0]
    copies = []
    for side, start in enumerate((depth - 2, 0)):
        for tile in range(tiles):
            copy = pltpu.make_async_copy(
                field.at[:, pl.ds(start, 2), :, pl.ds(tile * LANES, LANES)],
                edge.at[side, :, :, tile, pl.ds(TOP, length), :],
                sems.at[side * tiles + tile],
            )
            copy.start()
            copies.append(copy)
    pairs = [
        ((side, c, layer), (c, start + layer))
        for side, start in enumerate((depth - 2, 0))
        for c in range(comps)
        for layer in range(2)
    ]
    fill_halo(edge, before, after, pairs, length)
    acc[...] = jnp.zeros_like(acc)
    nodes = lane_nodes()
    lane = lax.broadcasted_iota(jnp.int32, (8, LANES), 1)
    counts = []
    for side, table in enumerate((upper_table, lower_table)):
        found = jnp.int32(0)
        for b in range(bins):
            first_x = table[b, 0]
            hits[side, found] = b
            wanted = first_x < 0 if side == 0 else first_x > depth - 4
            found = found + wanted.astype(jnp.int32)
        counts.append(found)
    for copy in copies:
        copy.wait()
    for side, table in enumerate((upper_table, lower_table)):

        def one_bin(n, _, side=side, table=table):
            b = hits[side, n]
            first_x, first_y, first_z = table[b, 0], table[b, 1], table[b, 2]
            for slot in range(2):
                layer = first_x + 2 + slot if side == 0 else first_x + 2 - depth + slot
                valid = (layer >= 0) & (layer < 2)
                layer = jnp.clip(layer, 0, 1)
                for c in range(comps):
                    acc[side, slot, c, b // BLOCK] += gather_rows(
                        edge, (side, c, layer), first_y, first_z, b % BLOCK, nodes, lane, valid
                    )
            return 0

        lax.fori_loop(0, counts[side], one_bin, 0)
    for side, out in enumerate((upper_out, lower_out)):
        out[...] = jnp.zeros_like(out)
        for slot in range(2):
            for c in range(comps):
                for tile in range(bins // BLOCK):
                    out[tile, slot * 4 + c : slot * 4 + c + 1, :] = flatten_rows(acc[side, slot, c, tile])


def cubic(t, row_node):
    lead = jnp.where(row_node == 0, -1.0 / 6.0, jnp.where(row_node == 1, 0.5, jnp.where(row_node == 2, -0.5, 1.0 / 6.0)))
    first = jnp.where(row_node == 0, 0.0, -1.0)
    second = jnp.where(row_node <= 1, 1.0, 0.0)
    third = jnp.where(row_node == 3, 1.0, 2.0)
    return (lead * (t - first)) * ((t - second) * (t - third))


def sample(lhs, position, patterns):
    fine, low, high = patterns
    n = position.shape[1]
    px = jnp.broadcast_to(position[0:1], (8, n))
    py = jnp.broadcast_to(position[1:2], (8, n))
    pz = jnp.broadcast_to(position[2:3], (8, n))
    along_z = cubic(pz, fine)
    weights = jnp.concatenate([along_z * cubic(py, low), along_z * cubic(py, high)], axis=0)
    head = weights.astype(jnp.bfloat16)
    tail = (weights - head.astype(jnp.float32)).astype(jnp.bfloat16)
    planes = jnp.dot(lhs, jnp.concatenate([head, head, tail], axis=0), preferred_element_type=jnp.float32)
    total = planes[0:8] * cubic(px, low) + planes[8:16] * cubic(px, high)
    return total[0:4] + total[4:8]


def pack_box(table, slot):
    box = pltpu.roll(table, (LANES - NODES * slot) & (LANES - 1), 1)
    head = box.astype(jnp.bfloat16).astype(jnp.float32)
    tail = box - head
    lane = lax.broadcasted_iota(jnp.int32, box.shape, 1)
    packed = jnp.where(
        lane < NODES,
        head,
        jnp.where(lane < 2 * NODES, pltpu.roll(tail, NODES, 1), pltpu.roll(head, 2 * NODES, 1)),
    )
    return packed[:, : 3 * NODES].astype(jnp.bfloat16)


def advance_bins(bins, load_table, state, stokes, store):
    row = lax.broadcasted_iota(jnp.int32, (8, 1), 0)
    patterns = (row % 4, row // 4, 2 + row // 4)
    boxes = [pack_box(load_table(b // BLOCK), b % BLOCK) for b in bins]
    states = [state[b] for b in bins]
    rates = [1.0 / stokes[pl.ds(b, 1), :] for b in bins]
    carry = [(s[0:3], s[3:6]) for s in states]

    def substep(_, carry):
        moved = []
        for (position, velocity), box, rate in zip(carry, boxes, rates):
            middle_pos = position + 0.5 * STEP_SIZE * velocity
            here = sample(box, position, patterns)[0:3]
            there = sample(box, middle_pos, patterns)[0:3]
            slope = (here - velocity) * rate
            middle_vel = velocity + 0.5 * STEP_SIZE * slope
            moved.append(
                (position + STEP_SIZE * middle_vel, velocity + STEP_SIZE * (there - middle_vel) * rate)
            )
        return moved

    carry = lax.fori_loop(0, SUBSTEPS, substep, carry)
    for b, (position, velocity) in zip(bins, carry):
        store(b, position, velocity)


def main_kernel(
    table, live, field, before, after, state, stokes, out, box_table, late, padded, acc, early, sems
):
    comps, depth, length, cells = field.shape
    tiles = cells // LANES
    bins = table.shape[0]
    copies = []
    for tile in range(tiles):
        copy = pltpu.make_async_copy(
            field.at[:, :, :, pl.ds(tile * LANES, LANES)],
            padded.at[:, :, tile, pl.ds(TOP, length), :],
            sems.at[tile],
        )
        copy.start()
        copies.append(copy)
    fill_halo(padded, before, after, [((c, x), (c, x)) for c in range(comps) for x in range(depth)], length)
    out[...] = state[...]
    count = live[0]
    early_count, late_count = jnp.int32(0), jnp.int32(0)
    for b in range(bins):
        first_x = table[b, 0]
        alone = (first_x >= 0) & (first_x <= depth - 4)
        is_live = b < count
        early[early_count] = b
        late[late_count] = b
        early_count = early_count + (alone & is_live).astype(jnp.int32)
        late_count = late_count + (jnp.logical_not(alone) & is_live).astype(jnp.int32)
    late[bins] = late_count
    for copy in copies:
        copy.wait()
    nodes = lane_nodes()
    lane = lax.broadcasted_iota(jnp.int32, (8, LANES), 1)
    box_table[...] = jnp.zeros_like(box_table)

    def one_tile(tile, _):
        acc[...] = jnp.zeros_like(acc)

        def one_bin(slot, _):
            b = tile * BLOCK + slot
            first_x, first_y, first_z = table[b, 0], table[b, 1], table[b, 2]
            for i in range(4):
                x = first_x + i
                valid = (x >= 0) & (x < depth)
                x = jnp.clip(x, 0, depth - 1)
                for c in range(comps):
                    acc[i, c] += gather_rows(padded, (c, x), first_y, first_z, slot, nodes, lane, valid)
            return 0

        lax.fori_loop(0, BLOCK, one_bin, 0)
        for i in range(4):
            for c in range(comps):
                box_table[tile, i * 4 + c : i * 4 + c + 1, :] = flatten_rows(acc[i, c])
        return 0

    lax.fori_loop(0, (count + BLOCK - 1) // BLOCK, one_tile, 0)

    def store(b, position, velocity):
        out[b, 0:3] = position
        out[b, 3:6] = velocity

    def one_block(n, _):
        chosen = [early[jnp.minimum(n * BLOCK + k, early_count - 1)] for k in range(BLOCK)]
        advance_bins(chosen, lambda tile: box_table[tile], state, stokes, store)
        return 0

    lax.fori_loop(0, (early_count + BLOCK - 1) // BLOCK, one_block, 0)


def late_kernel(late, box_table, from_lower, from_upper, state, stokes, done, out, full):
    bins = state.shape[0]
    full[:, 0:8, :] = box_table[:, 0:8, :] + from_lower[...]
    full[:, 8:16, :] = box_table[:, 8:16, :] + from_upper[...]
    out[...] = done[...]
    count = late[bins]

    def store(b, position, velocity):
        out[b, 0:3] = position
        out[b, 3:6] = velocity

    def one_block(n, _):
        chosen = [late[jnp.minimum(n * BLOCK + k, count - 1)] for k in range(BLOCK)]
        advance_bins(chosen, lambda tile: full[tile], state, stokes, store)
        return 0

    lax.fori_loop(0, (count + BLOCK - 1) // BLOCK, one_block, 0)


def in_smem():
    return pl.BlockSpec(memory_space=pltpu.SMEM)


def in_vmem():
    return pl.BlockSpec(memory_space=pltpu.VMEM)


def in_place():
    return pl.BlockSpec(memory_space=pl.ANY)


def body(velocity_field, particle_state, stokes_time, box_base, live_bins):
    comps, depth, length, cells = velocity_field.shape
    bins = box_base.shape[0]
    tiles = cells // LANES
    groups = bins // BLOCK

    def shift(array, axis, step):
        devices = lax.axis_size(axis)
        return lax.ppermute(array, axis, [(i, (i + step) % devices) for i in range(devices)])

    before = shift(velocity_field[:, :, length - 2 :, :], "sub", 1)
    after = shift(velocity_field[:, :, :2, :], "sub", -1)
    upper_table = shift(box_base, "slab", -1)
    lower_table = shift(box_base, "slab", 1)

    answer = jax.ShapeDtypeStruct((groups, 8, LANES), jnp.float32)
    for_upper, for_lower = pl.pallas_call(
        answer_kernel,
        out_shape=(answer, answer),
        in_specs=[in_smem(), in_smem(), in_place(), in_vmem(), in_vmem()],
        out_specs=(in_vmem(), in_vmem()),
        scratch_shapes=[
            pltpu.VMEM((2, comps, 2, tiles, length + 2 * TOP, LANES), jnp.float32),
            pltpu.VMEM((2, 2, comps, groups, 8, LANES), jnp.float32),
            pltpu.SMEM((2, bins + 1), jnp.int32),
            pltpu.SemaphoreType.DMA((2 * tiles,)),
        ],
        compiler_params=pltpu.CompilerParams(vmem_limit_bytes=VMEM_LIMIT),
        name="answers",
    )(upper_table, lower_table, velocity_field, before, after)
    from_lower = shift(for_upper, "slab", 1)
    from_upper = shift(for_lower, "slab", -1)

    moved, box_table, late = pl.pallas_call(
        main_kernel,
        out_shape=(
            jax.ShapeDtypeStruct(particle_state.shape, jnp.float32),
            jax.ShapeDtypeStruct((groups, NODES, LANES), jnp.float32),
            jax.ShapeDtypeStruct((bins + 1,), jnp.int32),
        ),
        in_specs=[in_smem(), in_smem(), in_place(), in_vmem(), in_vmem(), in_vmem(), in_vmem()],
        out_specs=(in_vmem(), in_vmem(), in_smem()),
        scratch_shapes=[
            pltpu.VMEM((comps, depth, tiles, length + 2 * TOP, LANES), jnp.float32),
            pltpu.VMEM((4, comps, 8, LANES), jnp.float32),
            pltpu.SMEM((bins + 1,), jnp.int32),
            pltpu.SemaphoreType.DMA((tiles,)),
        ],
        compiler_params=pltpu.CompilerParams(vmem_limit_bytes=VMEM_LIMIT),
        cost_estimate=pl.CostEstimate(flops=10_000_000, bytes_accessed=4_000_000, transcendentals=0),
        name="own_bins",
    )(box_base, live_bins, velocity_field, before, after, particle_state, stokes_time)

    return pl.pallas_call(
        late_kernel,
        out_shape=jax.ShapeDtypeStruct(particle_state.shape, jnp.float32),
        in_specs=[in_smem()] + [in_vmem()] * 6,
        out_specs=in_vmem(),
        scratch_shapes=[pltpu.VMEM((groups, NODES, LANES), jnp.float32)],
        compiler_params=pltpu.CompilerParams(vmem_limit_bytes=VMEM_LIMIT),
        name="edge_bins",
    )(late, box_table, from_lower, from_upper, particle_state, stokes_time, moved)


def solution(mesh):
    placed = (
        P(None, "slab", "sub", None),
        P(("slab", "sub"), None, None),
        P(("slab", "sub"), None),
        P(("slab", "sub"), None),
        P(("slab", "sub")),
    )
    return jax.shard_map(
        body, mesh=mesh, in_specs=placed, out_specs=P(("slab", "sub"), None, None), check_vma=False
    )
```

time: 98 us -> 30.7 us (0.31)
  the two profiles are of different devices: /device:TPU:21 before, /device:TPU:0 now
where the time goes in v1:
time: 30.7 us; the launch traced here: 30.3 us
  Pallas kernels  11.5 us (37%)
  starting transfers between devices  11.2 us (36%)
  local copies, waits for them, and re-layouts  5.11 us (17%)
  waiting for transfers between devices  1.73 us (6%)
  between operations  0.74 us (2%)
    ppermute x6, starting transfers between devices, shift(): lax.ppermute(array, axis, [(i, (i + step) % devices) for i in range(devic...  11.2 us
    pallas_call x1, Pallas kernels, body(): pl.pallas_call(main_kernel, out_shape=(jax.ShapeDtypeStruct(particle_stat...  7.46 us
    unnamed x10, local copies, waits for them, and re-layouts  2.78 us
    pallas_call x1, Pallas kernels, body(): pl.pallas_call(answer_kernel, out_shape=(answer, answer), in_specs=[in_sm...  2.17 us
    pallas_call x1, Pallas kernels, body(): pl.pallas_call(late_kernel, out_shape=jax.ShapeDtypeStruct(particle_state...  1.89 us
    ppermute x6, waiting for transfers between devices, shift(): lax.ppermute(array, axis, [(i, (i + step) % devices) for i in range(devic...  1.73 us
    slice x1, local copies, waits for them, and re-layouts, body(): after = shift(velocity_field[:, :, :2, :], 'sub', -1)  1.59 us
    pallas_call x1, local copies, waits for them, and re-layouts, body(): pl.pallas_call(late_kernel, out_shape=jax.ShapeDtypeStruct(particle_state...  0.74 us
  transfers between devices with their start and end apart: 6, of which 1 were waited for; matrix products, arithmetic and copies ran while one was open for 3% of the time, Pallas kernels for 25%

profile of v1, /device:TPU:0, one launch (start us, length us, event | category | flops | bytes accessed | tf_op | source)
XLA Modules:
  0.0 30.3 jit_solution(16460760108748722523)
XLA Ops:
  0.0 1.6 %fusion = (f32[3,16,2,512]{3,2,1,0:T(2,128)S(1)}, f32[3,16,2,512]{3,2,1,0:T(2,128)S(1)}) fusion(f32[3,16,32,512]{3,2,1,0:T(8,128)} %field.3), kind=kLoop, calls=%fused_computation | loop fusion | bytes 786432 | tf_op jit(solution)/shard_map/slice | solution.py:284
  1.6 3.4 %collective-permute-start.1 = (f32[3,16,2,512]{3,2,1,0:T(2,128)S(1)}, f32[3,16,2,512]{3,2,1,0:T(2,128)S(1)}, u32[]{:S(2)}, u32[]{:S(2)}) collective-permute-start(f32[3,16,2,512]{3,2,1,0:T(2,128)S(1)} %get-tuple-element.15), channel_id=1, source_target_pairs={{0,7},{1,0},{2,1},{3,2},{4,3},{5,4},{6,5},{7,6},{8,15},{9,8},{10,9... | collective-permute-start | bytes 589832 | tf_op jit(solution)/shard_map/ppermute | solution.py:281
  5.0 0.0 collective-permute-start
  5.0 0.8 %copy.6.table = s32[32,3]{1,0:T(8,128)S(1)} copy(s32[32,3]{0,1:T(4,128)} %param.8) | data formatting | bytes 768 | tf_op args[3]
  5.8 1.6 %collective-permute-start.3 = (s32[32,3]{1,0:T(8,128)S(1)}, s32[32,3]{1,0:T(8,128)S(1)}, u32[]{:S(2)}, u32[]{:S(2)}) collective-permute-start(s32[32,3]{1,0:T(8,128)S(1)} %copy.6.table), channel_id=1, source_target_pairs={{0,8},{8,16},{16,24},{24,0},{1,9},{9,17},{17,25},{25,1},{2,10},{10... | collective-permute-start | bytes 1160 | tf_op jit(solution)/shard_map/ppermute | solution.py:281
  7.3 2.2 %collective-permute-start.2 = (s32[32,3]{1,0:T(8,128)S(1)}, s32[32,3]{1,0:T(8,128)S(1)}, u32[]{:S(2)}, u32[]{:S(2)}) collective-permute-start(s32[32,3]{1,0:T(8,128)S(1)} %copy.6.table), channel_id=1, source_target_pairs={{0,24},{8,0},{16,8},{24,16},{1,25},{9,1},{17,9},{25,17},{2,26},{10... | collective-permute-start | bytes 1160 | tf_op jit(solution)/shard_map/ppermute | solution.py:281
  9.6 1.7 %collective-permute-done.3.lower_table = s32[32,3]{1,0:T(8,128)S(1)} collective-permute-done((s32[32,3]{1,0:T(8,128)S(1)}, s32[32,3]{1,0:T(8,128)S(1)}, u32[]{:S(2)}, u32[]{:S(2)}) %collective-permute-start.3) | collective-permute-done | bytes 416 | tf_op jit(solution)/shard_map/ppermute | solution.py:281
  11.3 0.0 collective-permute-done.2.upper_table
  11.3 0.0 collective-permute-done.1.after
  11.3 0.0 collective-permute-done.before
  11.3 0.0 copy-start
  11.3 1.9 %copy-done = f32[3,16,32,512]{3,2,1,0:T(8,128)S(1)} copy-done((f32[3,16,32,512]{3,2,1,0:T(8,128)S(1)}, f32[3,16,32,512]{3,2,1,0:T(8,128)}, u32[]{:S(2)}) %copy-start) | copy-done | bytes 3145752
  13.2 2.2 %answers.1 = (f32[4,8,128]{2,1,0:T(8,128)S(1)}, f32[4,8,128]{2,1,0:T(8,128)S(1)}) custom-call(s32[32,3]{1,0:T(8,128)S(1)} %collective-permute-done.2.upper_table, s32[32,3]{1,0:T(8,128)S(1)} %collective-permute-done.3.lower_table, f32[3,16,32,512]{3,2,1,0:T(8,128)S(1)} %copy-done, f32[3,16,2,512]{3,2,1,0:T(2,128)S(1)} %collective-permute-done.before, ...), custom_call_target="tpu_custom_call" | custom-call | tf_op jit(solution)/shard_map/answers/pallas_call | solution.py:289
  15.4 1.5 %collective-permute-start.4 = (f32[4,8,128]{2,1,0:T(8,128)S(1)}, f32[4,8,128]{2,1,0:T(8,128)S(1)}, u32[]{:S(2)}, u32[]{:S(2)}) collective-permute-start(f32[4,8,128]{2,1,0:T(8,128)S(1)} %get-tuple-element.12), channel_id=1, source_target_pairs={{0,8},{8,16},{16,24},{24,0},{1,9},{9,17},{17,25},{25,1},{2,10},{10... | collective-permute-start | bytes 49160 | tf_op jit(solution)/shard_map/ppermute | solution.py:281
  16.9 2.5 %collective-permute-start.5 = (f32[4,8,128]{2,1,0:T(8,128)S(1)}, f32[4,8,128]{2,1,0:T(8,128)S(1)}, u32[]{:S(2)}, u32[]{:S(2)}) collective-permute-start(f32[4,8,128]{2,1,0:T(8,128)S(1)} %get-tuple-element.13), channel_id=1, source_target_pairs={{0,24},{8,0},{16,8},{24,16},{1,25},{9,1},{17,9},{25,17},{2,26},{10... | collective-permute-start | bytes 49160 | tf_op jit(solution)/shard_map/ppermute | solution.py:281
  20.0 0.0 copy-done.3
  20.1 0.1 copy.7.state
  20.2 0.0 copy-done.2
  20.2 0.0 copy-done.1
  20.2 7.5 %own_bins.1 = (f32[32,6,256]{2,1,0:T(8,128)S(1)}, f32[4,16,128]{2,1,0:T(8,128)S(1)}, s32[33]{0:T(128)S(1)}) custom-call(s32[32,3]{1,0:T(8,128)S(1)} %copy.6.table, s32[1]{0:T(128)S(6)} %copy.12.live, f32[3,16,32,512]{3,2,1,0:T(8,128)S(1)} %copy-done.1, f32[3,16,2,512]{3,2,1,0:T(2,128)S(1)} %collective-permute-done.before, ...), custom_call_target="tpu_custom_call" | custom-call | flops 10000000 | bytes 4000000 | tf_op jit(solution)/shard_map/own_bins/pallas_call | solution.py:306
  27.7 0.0 collective-permute-done.4.from_lower
  27.7 0.0 collective-permute-done.5.from_upper
  27.7 1.9 %edge_bins.1 = f32[32,6,256]{2,1,0:T(8,128)S(1)} custom-call(s32[33]{0:T(128)S(1)} %get-tuple-element.10.late, f32[4,16,128]{2,1,0:T(8,128)S(1)} %get-tuple-element.11.box_table, f32[4,8,128]{2,1,0:T(8,128)S(1)} %collective-permute-done.4.from_lower, f32[4,8,128]{2,1,0:T(8,128)S(1)} %collective-permute-done.5.from_upper, f32[32,6,256]{2,1,0:T(8,128)S(1)} %copy.7.state, ...), custom_call_target="tpu_custom_call" | custom-call | tf_op jit(solution)/shard_map/edge_bins/pallas_call | solution.py:326
  29.6 0.7 %copy.11 = f32[32,6,256]{2,0,1:T(8,128)} copy(f32[32,6,256]{2,1,0:T(8,128)S(1)} %edge_bins.1) | data formatting | bytes 393216 | tf_op jit(solution)/shard_map/edge_bins/pallas_call | solution.py:326
  (3 shorter events, 0.0 us)
Async XLA Ops:
  0.0 20.0 %copy-start.3 = (f32[32,6,256]{2,0,1:T(8,128)S(1)}, f32[32,6,256]{2,0,1:T(8,128)}, u32[]{:S(2)}) copy-start(f32[32,6,256]{2,0,1:T(8,128)} %param.6) | copy-start | bytes 589828
  0.0 20.2 %copy-start.2 = (f32[32,256]{1,0:T(8,128)S(1)}, f32[32,256]{1,0:T(8,128)}, u32[]{:S(2)}) copy-start(f32[32,256]{1,0:T(8,128)} %stokes.3) | copy-start | bytes 98308
  1.6 9.7 %collective-permute-start.1 = (f32[3,16,2,512]{3,2,1,0:T(2,128)S(1)}, f32[3,16,2,512]{3,2,1,0:T(2,128)S(1)}, u32[]{:S(2)}, u32[]{:S(2)}) collective-permute-start(f32[3,16,2,512]{3,2,1,0:T(2,128)S(1)} %get-tuple-element.15), channel_id=1, source_target_pairs={{0,7},{1,0},{2,1},{3,2},{4,3},{5,4},{6,5},{7,6},{8,15},{9,8},{10,9... | collective-permute-start | bytes 589832 | tf_op jit(solution)/shard_map/ppermute | solution.py:281
  5.0 6.3 %collective-permute-start = (f32[3,16,2,512]{3,2,1,0:T(2,128)S(1)}, f32[3,16,2,512]{3,2,1,0:T(2,128)S(1)}, u32[]{:S(2)}, u32[]{:S(2)}) collective-permute-start(f32[3,16,2,512]{3,2,1,0:T(2,128)S(1)} %get-tuple-element.16), channel_id=1, source_target_pairs={{0,1},{1,2},{2,3},{3,4},{4,5},{5,6},{6,7},{7,0},{8,9},{9,10},{10,1... | collective-permute-start | bytes 589832 | tf_op jit(solution)/shard_map/ppermute | solution.py:281
  5.8 5.5 %collective-permute-start.3 = (s32[32,3]{1,0:T(8,128)S(1)}, s32[32,3]{1,0:T(8,128)S(1)}, u32[]{:S(2)}, u32[]{:S(2)}) collective-permute-start(s32[32,3]{1,0:T(8,128)S(1)} %copy.6.table), channel_id=1, source_target_pairs={{0,8},{8,16},{16,24},{24,0},{1,9},{9,17},{17,25},{25,1},{2,10},{10... | collective-permute-start | bytes 1160 | tf_op jit(solution)/shard_map/ppermute | solution.py:281
  7.3 4.0 %collective-permute-start.2 = (s32[32,3]{1,0:T(8,128)S(1)}, s32[32,3]{1,0:T(8,128)S(1)}, u32[]{:S(2)}, u32[]{:S(2)}) collective-permute-start(s32[32,3]{1,0:T(8,128)S(1)} %copy.6.table), channel_id=1, source_target_pairs={{0,24},{8,0},{16,8},{24,16},{1,25},{9,1},{17,9},{25,17},{2,26},{10... | collective-permute-start | bytes 1160 | tf_op jit(solution)/shard_map/ppermute | solution.py:281
  11.3 1.9 %copy-start = (f32[3,16,32,512]{3,2,1,0:T(8,128)S(1)}, f32[3,16,32,512]{3,2,1,0:T(8,128)}, u32[]{:S(2)}) copy-start(f32[3,16,32,512]{3,2,1,0:T(8,128)} %field.3) | copy-start | bytes 9437188
  13.2 7.0 %copy-start.1 = (f32[3,16,32,512]{3,2,1,0:T(8,128)S(1)}, f32[3,16,32,512]{3,2,1,0:T(8,128)}, u32[]{:S(2)}) copy-start(f32[3,16,32,512]{3,2,1,0:T(8,128)} %field.3) | copy-start | bytes 9437188
  15.4 12.3 %collective-permute-start.4 = (f32[4,8,128]{2,1,0:T(8,128)S(1)}, f32[4,8,128]{2,1,0:T(8,128)S(1)}, u32[]{:S(2)}, u32[]{:S(2)}) collective-permute-start(f32[4,8,128]{2,1,0:T(8,128)S(1)} %get-tuple-element.12), channel_id=1, source_target_pairs={{0,8},{8,16},{16,24},{24,0},{1,9},{9,17},{17,25},{25,1},{2,10},{10... | collective-permute-start | bytes 49160 | tf_op jit(solution)/shard_map/ppermute | solution.py:281
  16.9 10.8 %collective-permute-start.5 = (f32[4,8,128]{2,1,0:T(8,128)S(1)}, f32[4,8,128]{2,1,0:T(8,128)S(1)}, u32[]{:S(2)}, u32[]{:S(2)}) collective-permute-start(f32[4,8,128]{2,1,0:T(8,128)S(1)} %get-tuple-element.13), channel_id=1, source_target_pairs={{0,24},{8,0},{16,8},{24,16},{1,25},{9,1},{17,9},{25,17},{2,26},{10... | collective-permute-start | bytes 49160 | tf_op jit(solution)/shard_map/ppermute | solution.py:281

commit v2 on v0

v2 whole, which is shorter than its diff:
```python
import functools

import jax
import jax.numpy as jnp
from jax import lax
from jax.experimental import pallas as pl
from jax.experimental.pallas import tpu as pltpu
from jax.sharding import PartitionSpec as P

SUBSTEPS = 4
STEP_SIZE = 0.2
LANES = 128
NODES = 16
GROUP = 8
TOP = 8
ANSWERS = 4
VMEM_LIMIT = 48 * 1024 * 1024


def rows_and_lanes():
    return lax.broadcasted_iota(jnp.int32, (8, LANES), 0), lax.broadcasted_iota(jnp.int32, (8, LANES), 1)


def gather_pair(planes, index, valid, nodes, first_row, first_z, slot):
    row, lane = rows_and_lanes()
    tiles = planes.shape[-3]
    tile, offset = first_z // LANES, first_z % LANES
    beside = (tile + 1) % tiles
    upper = row < 4
    first, second = index

    def load(at):
        return jnp.where(
            upper,
            planes[(*first, at, pl.ds(first_row, 8), slice(None))],
            planes[(*second, at, pl.ds(first_row - 4, 8), slice(None))],
        )

    rows = jnp.where(lane >= offset, load(tile), load(beside))
    rows = pltpu.roll(rows, (NODES * slot - first_z) & (LANES - 1), 1)
    wanted = jnp.where(upper, jnp.where(valid[0], 4 * slot, -1), jnp.where(valid[1], 4 * slot, -1))
    return rows, nodes & (lane // 4 == wanted)


def flatten_pair(parts):
    row, _ = rows_and_lanes()
    total = None
    for c, part in enumerate(parts):
        part = pltpu.roll(part, 0, 1, stride=4, stride_axis=0)
        part = part + pltpu.roll(part, 7, 0)
        part = part + pltpu.roll(part, 6, 0)
        part = jnp.where(row % 4 == 0, part, 0.0)
        part = pltpu.roll(part, c, 0) if c else part
        total = part if total is None else total + part
    return total


def align_pair(tile):
    row, _ = rows_and_lanes()
    return jnp.where(row < 4, tile, pltpu.roll(tile, LANES - NODES, 1))


def load_kernel(field, padded, near, far, sems):
    comps, depth, length, cells = field.shape
    tiles = cells // LANES
    copies = []
    for tile in range(tiles):
        copy = pltpu.make_async_copy(
            field.at[:, :, :, pl.ds(tile * LANES, LANES)],
            padded.at[:, :, tile, pl.ds(TOP, length), :],
            sems.at[tile],
        )
        copy.start()
        copies.append(copy)
    even = lax.axis_index("sub") % 2 == 0
    first, last = TOP, TOP + length - 2
    near_row, far_row = jnp.where(even, last, first), jnp.where(even, first, last)
    for tile in range(tiles):
        copies[tile].wait()
        lanes = slice(tile * LANES, (tile + 1) * LANES)
        for c in range(comps):
            for x in range(depth):
                near[c, x, :, lanes] = padded[c, x, tile, pl.ds(near_row, 2), :]
                far[c, x, :, lanes] = padded[c, x, tile, pl.ds(far_row, 2), :]


def fill_halo(halo, near, far, planes):
    even = lax.axis_index("sub") % 2 == 0
    near_row, far_row = jnp.where(even, 8, 6), jnp.where(even, 6, 8)
    for c in range(halo.shape[0]):
        for into, x in enumerate(planes):
            for tile in range(halo.shape[-3]):
                lanes = slice(tile * LANES, (tile + 1) * LANES)
                halo[c, into, tile, pl.ds(near_row, 2), :] = near[c, x, :, lanes]
                halo[c, into, tile, pl.ds(far_row, 2), :] = far[c, x, :, lanes]


def halo_row(first_y, length):
    return jnp.where(first_y < 0, 8 + first_y, 8 + first_y - length)


def own_nodes(first_y, length):
    row, _ = rows_and_lanes()
    node = row % 4 + first_y
    return (node >= 0) & (node < length)


def box_planes(first_x, pair, depth):
    x = [first_x + 2 * pair, first_x + 2 * pair + 1]
    return [jnp.clip(at, 0, depth - 1) for at in x], [(at >= 0) & (at < depth) for at in x]


def own_boxes_kernel(table, live, padded, box_table):
    comps, depth, _, rows, _ = padded.shape
    length = rows - 2 * TOP
    box_table[...] = jnp.zeros_like(box_table)

    def one_group(group, _):
        parts = [[jnp.zeros((8, LANES), jnp.float32)] * comps for _ in range(2)]
        for slot in range(GROUP):
            b = group * GROUP + slot
            first_x, first_y, first_z = table[0, b], table[1, b], table[2, b]
            nodes = own_nodes(first_y, length)
            for pair in range(2):
                x, valid = box_planes(first_x, pair, depth)
                for c in range(comps):
                    found, mask = gather_pair(
                        padded, ((c, x[0]), (c, x[1])), valid, nodes, TOP + first_y, first_z, slot
                    )
                    parts[pair][c] = jnp.where(mask, found, parts[pair][c])
        for pair in range(2):
            box_table[group, 8 * pair : 8 * pair + 8, :] = align_pair(flatten_pair(parts[pair]))
        return 0

    lax.fori_loop(0, (live[0] + GROUP - 1) // GROUP, one_group, 0)


def halo_boxes_kernel(table, live, near, far, partial, box_table, halo, hits, *, length):
    comps, depth = near.shape[:2]
    bins = table.shape[1]
    found = jnp.int32(0)
    for b in range(bins):
        hits[found] = b
        crossing = (table[1, b] < 0) | (table[1, b] > length - 4)
        found = found + (crossing & (b < live[0])).astype(jnp.int32)
    box_table[...] = partial[...]
    fill_halo(halo, near, far, range(depth))

    def one_bin(n, _):
        b = hits[n]
        first_x, first_y, first_z = table[0, b], table[1, b], table[2, b]
        nodes = jnp.logical_not(own_nodes(first_y, length))
        for pair in range(2):
            x, valid = box_planes(first_x, pair, depth)
            parts = []
            for c in range(comps):
                rows, mask = gather_pair(
                    halo,
                    ((c, x[0]), (c, x[1])),
                    valid,
                    nodes,
                    halo_row(first_y, length),
                    first_z,
                    b % GROUP,
                )
                parts.append(jnp.where(mask, rows, 0.0))
            box_table[b // GROUP, 8 * pair : 8 * pair + 8, :] += align_pair(flatten_pair(parts))
        return 0

    lax.fori_loop(0, found, one_bin, 0)


def answers_kernel(near_table, far_table, padded, near, far, near_out, far_out, halo, acc, hits, crossing_hits):
    comps, depth, _, rows, _ = padded.shape
    length = rows - 2 * TOP
    bins = near_table.shape[1]
    groups = bins // GROUP
    even = lax.axis_index("slab") % 2 == 0
    acc[...] = jnp.zeros_like(acc)
    edge = [0, 1, depth - 2, depth - 1]
    found, crossing_found = jnp.int32(0), jnp.int32(0)
    for side, table in enumerate((near_table, far_table)):
        above = even if side == 0 else jnp.logical_not(even)
        for b in range(bins):
            first_x, first_y = table[0, b], table[1, b]
            wanted = jnp.where(above, first_x < 0, first_x > depth - 4)
            crossing = wanted & ((first_y < 0) | (first_y > length - 4))
            hits[found] = side * bins + b
            crossing_hits[crossing_found] = side * bins + b
            found = found + wanted.astype(jnp.int32)
            crossing_found = crossing_found + crossing.astype(jnp.int32)
    fill_halo(halo, near, far, edge)

    def one_bin(entry, used, planes, in_halo):
        side, b = entry // bins, entry % bins
        first_x, first_y, first_z = [jnp.where(side == 0, near_table[d, b], far_table[d, b]) for d in range(3)]
        above = (side == 0) == even
        x = first_x + jnp.where(above, depth, 2 - depth)
        x = [x, x + 1]
        valid = [used & (at >= 0) & (at < depth) for at in x]
        x = [jnp.clip(at, 0, depth - 1) for at in x]
        nodes = own_nodes(first_y, length)
        first_row = TOP + first_y
        if in_halo:
            x = [jnp.where(at < 2, at, jnp.maximum(at - (depth - 4), 2)) for at in x]
            nodes = jnp.logical_not(nodes)
            first_row = halo_row(first_y, length)
        parts = []
        for c in range(comps):
            gathered, mask = gather_pair(planes, ((c, x[0]), (c, x[1])), valid, nodes, first_row, first_z, b % GROUP)
            parts.append(jnp.where(mask, gathered, 0.0))
        acc[side * groups + b // GROUP] += flatten_pair(parts)

    def some_bins(n, _):
        for k in range(ANSWERS):
            at = n * ANSWERS + k
            one_bin(hits[jnp.minimum(at, found - 1)], at < found, padded, False)
        return 0

    def crossing_bin(n, _):
        one_bin(crossing_hits[n], True, halo, True)
        return 0

    lax.fori_loop(0, (found + ANSWERS - 1) // ANSWERS, some_bins, 0)
    lax.fori_loop(0, crossing_found, crossing_bin, 0)
    for g in range(groups):
        near_out[g] = align_pair(acc[g])
        far_out[g] = align_pair(acc[groups + g])


def unscaled_weights(t):
    plus, minus, minus_two = t + 1.0, t - 1.0, t - 2.0
    inner, outer = t * minus, plus * minus_two
    return inner * minus_two, outer * minus, outer * t, inner * plus


def node_factor(node):
    return jnp.where(node == 0, -1.0 / 6.0, jnp.where(node == 1, 0.5, jnp.where(node == 2, -0.5, 1.0 / 6.0)))


def split(x):
    head = x.astype(jnp.bfloat16)
    return head, (x - head.astype(jnp.float32)).astype(jnp.bfloat16)


def group_matrix(box):
    row = lax.broadcasted_iota(jnp.int32, box.shape, 0)
    lane = lax.broadcasted_iota(jnp.int32, box.shape, 1)
    box = box * (node_factor(row // 4) * node_factor(lane // 4 % 4) * node_factor(lane % 4))
    box = jnp.take_along_axis(box, lane % GROUP * NODES + lane // GROUP, axis=1)
    head = box.astype(jnp.bfloat16).astype(jnp.float32)
    own = lax.broadcasted_iota(jnp.int32, (GROUP, LANES), 1) % GROUP == lax.broadcasted_iota(
        jnp.int32, (GROUP, LANES), 0
    )

    def spread(part):
        rows = [
            jnp.where(own, jnp.broadcast_to(part[4 * i + c : 4 * i + c + 1], (GROUP, LANES)), 0.0)
            for i in range(4)
            for c in range(3)
        ]
        return jnp.concatenate(rows, axis=0).astype(jnp.bfloat16)

    heads, tails = spread(head), spread(box - head)
    return jnp.concatenate([heads, heads, tails], axis=1)


def sample(matrix, position):
    along_x, along_y, along_z = (unscaled_weights(t) for t in position)
    weights = jnp.concatenate([y * z for y in along_y for z in along_z], axis=0)
    head, tail = split(weights)
    planes = jnp.dot(
        matrix, jnp.concatenate([head, tail, head], axis=0), preferred_element_type=jnp.float32
    )
    result = []
    for c in range(3):
        plane = [planes[8 * (3 * i + c) : 8 * (3 * i + c) + 8] for i in range(4)]
        result.append(
            (plane[0] * along_x[0] + plane[1] * along_x[1]) + (plane[2] * along_x[2] + plane[3] * along_x[3])
        )
    return result


def move_kernel(live, box_table, from_near, from_far, state, stokes, out):
    groups = box_table.shape[0]
    count = live[0]
    even = lax.axis_index("slab") % 2 == 0
    matrices, carry, rates, alive = [], [], [], []
    for g in range(groups):
        rows = slice(g * GROUP, (g + 1) * GROUP)
        lower, upper = jnp.where(even, from_far[g], from_near[g]), jnp.where(even, from_near[g], from_far[g])
        answers = jnp.concatenate([lower, upper], axis=0)
        matrices.append(group_matrix(box_table[g] + answers))
        rates.append(1.0 / stokes[rows, :])
        kept = g * GROUP + lax.broadcasted_iota(jnp.int32, rates[g].shape, 0) < count
        alive.append(kept)
        start = [jnp.where(kept, state[c, rows, :], 0.0) for c in range(6)]
        carry.append((start[:3], start[3:]))

    for _ in range(SUBSTEPS):
        moved = []
        for g in range(groups):
            position, velocity = carry[g]
            rate = rates[g]
            middle_pos = [x + 0.5 * STEP_SIZE * v for x, v in zip(position, velocity)]
            here = sample(matrices[g], position)
            there = sample(matrices[g], middle_pos)
            middle_vel = [v + 0.5 * STEP_SIZE * ((u - v) * rate) for u, v in zip(here, velocity)]
            moved.append(
                (
                    [x + STEP_SIZE * m for x, m in zip(position, middle_vel)],
                    [v + STEP_SIZE * (u - m) * rate for v, u, m in zip(velocity, there, middle_vel)],
                )
            )
        carry = moved
    for g in range(groups):
        rows = slice(g * GROUP, (g + 1) * GROUP)
        for c, value in enumerate([*carry[g][0], *carry[g][1]]):
            out[c, rows, :] = jnp.where(alive[g], value, state[c, rows, :])


def in_smem():
    return pl.BlockSpec(memory_space=pltpu.SMEM)


def in_vmem():
    return pl.BlockSpec(memory_space=pltpu.VMEM)


def exchange(near, far, axis):
    devices = lax.axis_size(axis)
    near_pairs = [(i, i ^ 1) for i in range(devices)]
    far_pairs = [(i, (i + 1 if i % 2 else i - 1) % devices) for i in range(devices)]
    return lax.ppermute(near, axis, near_pairs), lax.ppermute(far, axis, far_pairs)


def body(velocity_field, particle_state, stokes_time, box_base, live_bins):
    comps, depth, length, cells = velocity_field.shape
    bins = box_base.shape[0]
    tiles = cells // LANES
    groups = bins // GROUP
    table = box_base.T
    state = particle_state.transpose(1, 0, 2)
    block = pltpu.with_memory_space_constraint(velocity_field, pltpu.HBM)
    params = pltpu.CompilerParams(vmem_limit_bytes=VMEM_LIMIT)

    near_table, far_table = exchange(table, table, "slab")
    edge_rows = jax.ShapeDtypeStruct((comps, depth, 2, cells), jnp.float32)
    padded, near, far = pl.pallas_call(
        load_kernel,
        out_shape=(pltpu.VMEM((comps, depth, tiles, length + 2 * TOP, LANES), jnp.float32), edge_rows, edge_rows),
        in_specs=[pl.BlockSpec(memory_space=pl.ANY)],
        out_specs=(in_vmem(), in_vmem(), in_vmem()),
        scratch_shapes=[pltpu.SemaphoreType.DMA((tiles,))],
        compiler_params=params,
        cost_estimate=pl.CostEstimate(flops=1_000_000, bytes_accessed=4_000_000, transcendentals=0),
        name="load",
    )(block)
    near, far = exchange(near, far, "sub")

    box_tables = jax.ShapeDtypeStruct((groups, NODES, LANES), jnp.float32)
    box_table = pl.pallas_call(
        own_boxes_kernel,
        out_shape=box_tables,
        in_specs=[in_smem(), in_smem(), in_vmem()],
        out_specs=in_vmem(),
        compiler_params=params,
        cost_estimate=pl.CostEstimate(flops=1_000_000, bytes_accessed=8_000_000, transcendentals=0),
        name="own_boxes",
    )(table, live_bins, padded)

    answer = jax.ShapeDtypeStruct((groups, 8, LANES), jnp.float32)
    near_answer, far_answer = pl.pallas_call(
        answers_kernel,
        out_shape=(answer, answer),
        in_specs=[in_smem(), in_smem(), in_vmem(), in_vmem(), in_vmem()],
        out_specs=(in_vmem(), in_vmem()),
        scratch_shapes=[
            pltpu.VMEM((comps, 4, tiles, 16, LANES), jnp.float32),
            pltpu.VMEM((2 * groups, 8, LANES), jnp.float32),
            pltpu.SMEM((2 * bins + 1,), jnp.int32),
            pltpu.SMEM((2 * bins + 1,), jnp.int32),
        ],
        compiler_params=params,
        name="answers",
    )(near_table, far_table, padded, near, far)
    from_near, from_far = exchange(near_answer, far_answer, "slab")

    box_table = pl.pallas_call(
        functools.partial(halo_boxes_kernel, length=length),
        out_shape=box_tables,
        in_specs=[in_smem(), in_smem(), in_vmem(), in_vmem(), in_vmem()],
        out_specs=in_vmem(),
        scratch_shapes=[
            pltpu.VMEM((comps, depth, tiles, 16, LANES), jnp.float32),
            pltpu.SMEM((bins + 1,), jnp.int32),
        ],
        compiler_params=params,
        cost_estimate=pl.CostEstimate(flops=1_000_000, bytes_accessed=4_000_000, transcendentals=0),
        name="halo_boxes",
    )(table, live_bins, near, far, box_table)

    moved = pl.pallas_call(
        move_kernel,
        out_shape=jax.ShapeDtypeStruct(state.shape, jnp.float32),
        in_specs=[in_smem()] + [in_vmem()] * 5,
        out_specs=in_vmem(),
        compiler_params=params,
        name="move",
    )(live_bins, box_table, from_near, from_far, state, stokes_time)
    return moved.transpose(1, 0, 2)


def solution(mesh):
    placed = (
        P(None, "slab", "sub", None),
        P(("slab", "sub"), None, None),
        P(("slab", "sub"), None),
        P(("slab", "sub"), None),
        P(("slab", "sub")),
    )
    return jax.shard_map(
        body, mesh=mesh, in_specs=placed, out_specs=P(("slab", "sub"), None, None), check_vma=False
    )
```

time: 98 us -> 23.5 us (0.24)
  the two profiles are of different devices: /device:TPU:21 before, /device:TPU:0 now
where the time goes in v2:
time: 23.5 us; the launch traced here: 23.3 us
  starting transfers between devices  10.8 us (46%)
  Pallas kernels  8.42 us (36%)
  waiting for transfers between devices  3.39 us (14%)
  between operations  0.7 us (3%)
    ppermute x3, starting transfers between devices, exchange(): lax.ppermute(far, axis, far_pairs)  8.66 us
    ppermute x3, waiting for transfers between devices, exchange(): lax.ppermute(far, axis, far_pairs)  3.38 us
    pallas_call x1, Pallas kernels, body(): pl.pallas_call(move_kernel, out_shape=jax.ShapeDtypeStruct(state.shape, j...  2.43 us
    ppermute x3, starting transfers between devices, exchange(): lax.ppermute(near, axis, near_pairs)  2.11 us
    pallas_call x1, Pallas kernels, body(): pl.pallas_call(load_kernel, out_shape=(pltpu.VMEM((comps, depth, tiles, l...  2 us
    pallas_call x1, Pallas kernels, body(): pl.pallas_call(answers_kernel, out_shape=(answer, answer), in_specs=[in_s...  1.95 us
    pallas_call x1, Pallas kernels, body(): pl.pallas_call(functools.partial(halo_boxes_kernel, length=length), out_s...  1.03 us
    pallas_call x1, Pallas kernels, body(): pl.pallas_call(own_boxes_kernel, out_shape=box_tables, in_specs=[in_smem(...  1 us
  transfers between devices with their start and end apart: 6, of which 2 were waited for; matrix products, arithmetic and copies ran while one was open for 0% of the time, Pallas kernels for 9%

profile of v2, /device:TPU:0, one launch (start us, length us, event | category | flops | bytes accessed | tf_op | source)
XLA Modules:
  0.0 23.3 jit_solution(11195062033366104736)
XLA Ops:
  0.0 0.0 copy-start.2
  0.0 2.0 %load.1 = (f32[3,16,4,48,128]{4,3,2,1,0:T(8,128)S(1)}, f32[3,16,2,512]{3,2,1,0:T(2,128)S(1)}, f32[3,16,2,512]{3,2,1,0:T(2,128)S(1)}) custom-call(f32[3,16,32,512]{3,2,1,0:T(8,128)} %field.1), custom_call_target="tpu_custom_call" | custom-call | flops 1000000 | bytes 4000000 | tf_op jit(solution)/shard_map/load/pallas_call | solution.py:349
  2.0 0.5 %collective-permute-start = (f32[3,16,2,512]{3,2,1,0:T(2,128)S(1)}, f32[3,16,2,512]{3,2,1,0:T(2,128)S(1)}, u32[]{:S(2)}, u32[]{:S(2)}) collective-permute-start(f32[3,16,2,512]{3,2,1,0:T(2,128)S(1)} %get-tuple-element.10), channel_id=1, source_target_pairs={{0,1},{1,0},{2,3},{3,2},{4,5},{5,4},{6,7},{7,6},{8,9},{9,8},{10,11... | collective-permute-start | bytes 589832 | tf_op jit(solution)/shard_map/ppermute | solution.py:334
  2.5 3.6 %collective-permute-start.1 = (f32[3,16,2,512]{3,2,1,0:T(2,128)S(1)}, f32[3,16,2,512]{3,2,1,0:T(2,128)S(1)}, u32[]{:S(2)}, u32[]{:S(2)}) collective-permute-start(f32[3,16,2,512]{3,2,1,0:T(2,128)S(1)} %get-tuple-element.11), channel_id=1, source_target_pairs={{0,7},{1,2},{2,1},{3,4},{4,3},{5,6},{6,5},{7,0},{8,15},{9,10},{10,... | collective-permute-start | bytes 589832 | tf_op jit(solution)/shard_map/ppermute | solution.py:334
  6.1 1.6 %collective-permute-start.2 = (s32[3,32]{1,0:T(4,128)}, s32[3,32]{1,0:T(4,128)S(1)}, u32[]{:S(2)}, u32[]{:S(2)}) collective-permute-start(s32[3,32]{1,0:T(4,128)} %bitcast.4), channel_id=1, source_target_pairs={{0,8},{8,0},{16,24},{24,16},{1,9},{9,1},{17,25},{25,17},{2,10},{10... | collective-permute-start | bytes 1160 | tf_op jit(solution)/shard_map/ppermute | solution.py:334
  7.7 2.5 %collective-permute-start.3 = (s32[3,32]{1,0:T(4,128)}, s32[3,32]{1,0:T(4,128)S(1)}, u32[]{:S(2)}, u32[]{:S(2)}) collective-permute-start(s32[3,32]{1,0:T(4,128)} %bitcast.5), channel_id=1, source_target_pairs={{0,24},{8,16},{16,8},{24,0},{1,25},{9,17},{17,9},{25,1},{2,26},{10... | collective-permute-start | bytes 1160 | tf_op jit(solution)/shard_map/ppermute | solution.py:334
  10.1 0.0 collective-permute-done.2.near_table
  10.1 3.1 %collective-permute-done.3.far_table = s32[3,32]{1,0:T(4,128)S(1)} collective-permute-done((s32[3,32]{1,0:T(4,128)}, s32[3,32]{1,0:T(4,128)S(1)}, u32[]{:S(2)}, u32[]{:S(2)}) %collective-permute-start.3) | collective-permute-done | bytes 416 | tf_op jit(solution)/shard_map/ppermute | solution.py:334
  13.3 0.0 collective-permute-done.near
  13.3 0.0 collective-permute-done.1.far
  13.3 0.0 copy-start
  13.3 0.0 copy-start.1
  13.3 2.0 %answers.1 = (f32[4,8,128]{2,1,0:T(8,128)S(1)}, f32[4,8,128]{2,1,0:T(8,128)S(1)}) custom-call(s32[3,32]{1,0:T(4,128)S(1)} %collective-permute-done.2.near_table, s32[3,32]{1,0:T(4,128)S(1)} %collective-permute-done.3.far_table, f32[3,16,4,48,128]{4,3,2,1,0:T(8,128)S(1)} %get-tuple-element.12.padded, f32[3,16,2,512]{3,2,1,0:T(2,128)S(1)} %collective-permute-done.near, ...), custom_call_target="tpu_custom_call" | custom-call | tf_op jit(solution)/shard_map/answers/pallas_call | solution.py:373
  15.2 0.0 collective-permute-start.4
  15.3 2.6 %collective-permute-start.5 = (f32[4,8,128]{2,1,0:T(8,128)S(1)}, f32[4,8,128]{2,1,0:T(8,128)S(1)}, u32[]{:S(2)}, u32[]{:S(2)}) collective-permute-start(f32[4,8,128]{2,1,0:T(8,128)S(1)} %get-tuple-element.14), channel_id=1, source_target_pairs={{0,24},{8,16},{16,8},{24,0},{1,25},{9,17},{17,9},{25,1},{2,26},{10... | collective-permute-start | bytes 49160 | tf_op jit(solution)/shard_map/ppermute | solution.py:334
  18.5 0.0 copy-done.2
  18.6 1.0 %own_boxes.1.partial = f32[4,16,128]{2,1,0:T(8,128)S(1)} custom-call(s32[3,32]{1,0:T(4,128)S(1)} %bitcast.6, s32[1]{0:T(128)S(6)} %copy.6.live, f32[3,16,4,48,128]{4,3,2,1,0:T(8,128)S(1)} %get-tuple-element.12.padded), custom_call_target="tpu_custom_call" | custom-call | flops 1000000 | bytes 8000000 | tf_op jit(solution)/shard_map/own_boxes/pallas_call | solution.py:362
  19.6 1.0 %halo_boxes.1.box_table = f32[4,16,128]{2,1,0:T(8,128)S(1)} custom-call(s32[3,32]{1,0:T(4,128)S(1)} %bitcast.7, s32[1]{0:T(128)S(6)} %copy.6.live, f32[3,16,2,512]{3,2,1,0:T(2,128)S(1)} %collective-permute-done.near, f32[3,16,2,512]{3,2,1,0:T(2,128)S(1)} %collective-permute-done.1.far, f32[4,16,128]{2,1,0:T(8,128)S(1)} %own_boxes.1.partial), custom_call_target="tpu_custom_call" | custom-call | flops 1000000 | bytes 4000000 | tf_op jit(solution)/shard_map/halo_boxes/pallas_call | solution.py:389
  20.6 0.0 collective-permute-done.4.from_near
  20.6 0.3 %collective-permute-done.5.from_far = f32[4,8,128]{2,1,0:T(8,128)S(1)} collective-permute-done((f32[4,8,128]{2,1,0:T(8,128)S(1)}, f32[4,8,128]{2,1,0:T(8,128)S(1)}, u32[]{:S(2)}, u32[]{:S(2)}) %collective-permute-start.5) | collective-permute-done | bytes 16416 | tf_op jit(solution)/shard_map/ppermute | solution.py:334
  20.9 0.0 copy-done
  20.9 0.0 copy-done.1
  20.9 2.4 %move.1 = f32[6,32,256]{2,1,0:T(8,128)} custom-call(s32[1]{0:T(128)S(6)} %copy.6.live, f32[4,16,128]{2,1,0:T(8,128)S(1)} %halo_boxes.1.box_table, f32[4,8,128]{2,1,0:T(8,128)S(1)} %collective-permute-done.4.from_near, f32[4,8,128]{2,1,0:T(8,128)S(1)} %collective-permute-done.5.from_far, f32[6,32,256]{2,1,0:T(8,128)S(1)} %bitcast.3, f32[32,256]{1,0:T(8,128)S(1)} %copy-done.1), custom_call_target="tpu_custom_call" | custom-call | tf_op jit(solution)/shard_map/move/pallas_call | solution.py:403
Async XLA Ops:
  0.0 18.5 %copy-start.2 = (s32[32,3]{0,1:T(4,128)S(1)}, s32[32,3]{0,1:T(4,128)}, u32[]{:S(2)}) copy-start(s32[32,3]{0,1:T(4,128)} %param.8) | copy-start | bytes 1156
  2.0 11.2 %collective-permute-start = (f32[3,16,2,512]{3,2,1,0:T(2,128)S(1)}, f32[3,16,2,512]{3,2,1,0:T(2,128)S(1)}, u32[]{:S(2)}, u32[]{:S(2)}) collective-permute-start(f32[3,16,2,512]{3,2,1,0:T(2,128)S(1)} %get-tuple-element.10), channel_id=1, source_target_pairs={{0,1},{1,0},{2,3},{3,2},{4,5},{5,4},{6,7},{7,6},{8,9},{9,8},{10,11... | collective-permute-start | bytes 589832 | tf_op jit(solution)/shard_map/ppermute | solution.py:334
  2.5 10.7 %collective-permute-start.1 = (f32[3,16,2,512]{3,2,1,0:T(2,128)S(1)}, f32[3,16,2,512]{3,2,1,0:T(2,128)S(1)}, u32[]{:S(2)}, u32[]{:S(2)}) collective-permute-start(f32[3,16,2,512]{3,2,1,0:T(2,128)S(1)} %get-tuple-element.11), channel_id=1, source_target_pairs={{0,7},{1,2},{2,1},{3,4},{4,3},{5,6},{6,5},{7,0},{8,15},{9,10},{10,... | collective-permute-start | bytes 589832 | tf_op jit(solution)/shard_map/ppermute | solution.py:334
  6.1 4.1 %collective-permute-start.2 = (s32[3,32]{1,0:T(4,128)}, s32[3,32]{1,0:T(4,128)S(1)}, u32[]{:S(2)}, u32[]{:S(2)}) collective-permute-start(s32[3,32]{1,0:T(4,128)} %bitcast.4), channel_id=1, source_target_pairs={{0,8},{8,0},{16,24},{24,16},{1,9},{9,1},{17,25},{25,17},{2,10},{10... | collective-permute-start | bytes 1160 | tf_op jit(solution)/shard_map/ppermute | solution.py:334
  7.7 5.6 %collective-permute-start.3 = (s32[3,32]{1,0:T(4,128)}, s32[3,32]{1,0:T(4,128)S(1)}, u32[]{:S(2)}, u32[]{:S(2)}) collective-permute-start(s32[3,32]{1,0:T(4,128)} %bitcast.5), channel_id=1, source_target_pairs={{0,24},{8,16},{16,8},{24,0},{1,25},{9,17},{17,9},{25,1},{2,26},{10... | collective-permute-start | bytes 1160 | tf_op jit(solution)/shard_map/ppermute | solution.py:334
  13.3 7.6 %copy-start = (f32[32,6,256]{2,0,1:T(8,128)S(1)}, f32[32,6,256]{2,0,1:T(8,128)}, u32[]{:S(2)}) copy-start(f32[32,6,256]{2,0,1:T(8,128)} %param.6) | copy-start | bytes 589828
  13.3 7.6 %copy-start.1 = (f32[32,256]{1,0:T(8,128)S(1)}, f32[32,256]{1,0:T(8,128)}, u32[]{:S(2)}) copy-start(f32[32,256]{1,0:T(8,128)} %stokes.1) | copy-start | bytes 98308
  15.2 5.4 %collective-permute-start.4 = (f32[4,8,128]{2,1,0:T(8,128)S(1)}, f32[4,8,128]{2,1,0:T(8,128)S(1)}, u32[]{:S(2)}, u32[]{:S(2)}) collective-permute-start(f32[4,8,128]{2,1,0:T(8,128)S(1)} %get-tuple-element.13), channel_id=1, source_target_pairs={{0,8},{8,0},{16,24},{24,16},{1,9},{9,1},{17,25},{25,17},{2,10},{10... | collective-permute-start | bytes 49160 | tf_op jit(solution)/shard_map/ppermute | solution.py:334
  15.3 5.6 %collective-permute-start.5 = (f32[4,8,128]{2,1,0:T(8,128)S(1)}, f32[4,8,128]{2,1,0:T(8,128)S(1)}, u32[]{:S(2)}, u32[]{:S(2)}) collective-permute-start(f32[4,8,128]{2,1,0:T(8,128)S(1)} %get-tuple-element.14), channel_id=1, source_target_pairs={{0,24},{8,16},{16,8},{24,0},{1,25},{9,17},{17,9},{25,1},{2,26},{10... | collective-permute-start | bytes 49160 | tf_op jit(solution)/shard_map/ppermute | solution.py:334
